TPU v7x, 128 devices: a whole 4x4x4 slice. The times are simulated.
128 devices in a mesh: row: 16 (over z_hi, y, core), col: 8 (over z_lo, x).
Axes of the slice: x: 4, y: 4, z: 4 (z_hi: 2, z_lo: 2; z = z_hi * 2 + z_lo), core: 2. Of those that a mesh axis runs over, the one named last changes fastest.
Arguments:
- token_ids: int32 [16384], P(('row', 'col')), may hold values from 0 to 511
- embedding: bfloat16 [512, 8192], replicated, may hold values from -6 to 6
- norm_gain: bfloat16 [8192], replicated, may hold values from 0.099609375 to 1.8984375
- w_in: bfloat16 [8192, 12288], P(None, ('row', 'col')), may hold values from -0.0625 to 0.0625
- short_taps: float32 [7, 12288], replicated, may hold values from -2 to 2
- long_filter: float32 [16384, 4096], P(('row', 'col')), may hold values from -0.046875 to 0.046875
- skip_gain: float32 [4096], replicated, may hold values from -1 to 1
Outputs:
- mixed_out: bfloat16 [16384, 4096], P(('row', 'col'))
All inputs are finite; a program needn't handle non-finite values.
Results may differ from a plain program's by a relative error of at most 0.0095.
Values may be sent and summed in bfloat16 or wider, within the bound.
No kernel may reach another device: no remote copies, remote signals or barrier semaphores. Data moves between devices by JAX's collectives and lax.ppermute only.
A program may use at most 192 MiB of HBM per device.

v0:
```python
import math
import jax
import jax.numpy as jnp
from jax import lax
from jax.sharding import PartitionSpec as P

FFT_COLS = 128
EPSILON = 1e-05


def passed_along(x, axis, by):
    length = lax.axis_size(axis)
    pairs = [(i, i + by) for i in range(length) if 0 <= i + by < length]
    return lax.ppermute(x, axis, pairs)


def phase_table(first_index, second_index, period):
    turns = first_index * second_index % period
    return 2.0 * math.pi / period * turns.astype(jnp.float32)


def contract(form, table_part, data_part):
    return jnp.einsum(form, table_part, data_part, precision=lax.Precision.HIGHEST)


def project_table(embedding, norm_gain, w_in):
    rows_f32 = embedding.astype(jnp.float32)
    inverse_rms = lax.rsqrt(jnp.mean(rows_f32 * rows_f32, axis=1, keepdims=True) + EPSILON)
    normed = (rows_f32 * inverse_rms * norm_gain.astype(jnp.float32)).astype(jnp.bfloat16)
    own_columns = jnp.dot(normed, w_in, preferred_element_type=jnp.float32).astype(jnp.bfloat16)
    return lax.all_gather(own_columns, ("row", "col"), axis=1, tiled=True)


def short_filter(mixed_rows, short_taps):
    tap_count = short_taps.shape[0]
    row_count = mixed_rows.shape[0]
    earlier = passed_along(mixed_rows[row_count - (tap_count - 1) :], ("row", "col"), 1)
    extended = jnp.concatenate([earlier, mixed_rows], axis=0).astype(jnp.float32)
    result = short_taps[0] * extended[tap_count - 1 :]
    for offset in range(1, tap_count):
        begin_at = tap_count - 1 - offset
        result = result + short_taps[offset] * extended[begin_at : begin_at + row_count]
    return result


def local_causal(signal_all, filter_all):
    seq_len = signal_all.shape[0]
    width = signal_all.shape[1]
    short_len = seq_len // FFT_COLS
    first_len = 2 * short_len
    total_len = first_len * FFT_COLS
    angle_one = phase_table(
        lax.iota(jnp.int32, short_len)[:, None], lax.iota(jnp.int32, first_len)[None, :], first_len
    )
    cos_one = jnp.cos(angle_one)
    sin_one = jnp.sin(angle_one)
    angle_twist = phase_table(
        lax.iota(jnp.int32, first_len)[:, None], lax.iota(jnp.int32, FFT_COLS)[None, :], total_len
    )
    cos_twist = jnp.cos(angle_twist)
    sin_twist = jnp.sin(angle_twist)
    angle_two = phase_table(
        lax.iota(jnp.int32, FFT_COLS)[:, None], lax.iota(jnp.int32, FFT_COLS)[None, :], FFT_COLS
    )
    cos_two = jnp.cos(angle_two)
    sin_two = jnp.sin(angle_two)

    def forward(series):
        blocked = series.reshape(short_len, FFT_COLS, width)
        real_part = contract("sk,sjc->ckj", cos_one, blocked)
        imag_part = -contract("sk,sjc->ckj", sin_one, blocked)
        turned_re = real_part * cos_twist + imag_part * sin_twist
        turned_im = imag_part * cos_twist - real_part * sin_twist
        out_re = contract("jm,ckj->ckm", cos_two, turned_re) + contract(
            "jm,ckj->ckm", sin_two, turned_im
        )
        out_im = contract("jm,ckj->ckm", cos_two, turned_im) - contract(
            "jm,ckj->ckm", sin_two, turned_re
        )
        return (out_re, out_im)

    signal_re, signal_im = forward(signal_all)
    filter_re, filter_im = forward(filter_all)
    product_re = signal_re * filter_re - signal_im * filter_im
    product_im = signal_re * filter_im + signal_im * filter_re
    back_re = contract("jm,ckm->ckj", cos_two, product_re) - contract(
        "jm,ckm->ckj", sin_two, product_im
    )
    back_im = contract("jm,ckm->ckj", cos_two, product_im) + contract(
        "jm,ckm->ckj", sin_two, product_re
    )
    turned_re = back_re * cos_twist - back_im * sin_twist
    turned_im = back_im * cos_twist + back_re * sin_twist
    summed = contract("sk,ckj->sjc", cos_one, turned_re) - contract(
        "sk,ckj->sjc", sin_one, turned_im
    )
    return (summed * (1.0 / total_len)).reshape(seq_len, width)


def local(token_ids, embedding, norm_gain, w_in, short_taps, long_filter, skip_gain):
    lookup_table = project_table(embedding, norm_gain, w_in)
    vocab_size = lookup_table.shape[0]
    one_hot = (token_ids[:, None] == lax.iota(jnp.int32, vocab_size)[None, :]).astype(jnp.bfloat16)
    mixed_rows = jnp.dot(one_hot, lookup_table, preferred_element_type=jnp.float32).astype(
        jnp.bfloat16
    )
    filtered = short_filter(mixed_rows, short_taps)
    channels = filtered.shape[1] // 3
    gate_out = filtered[:, :channels]
    signal = filtered[:, channels : 2 * channels] * filtered[:, 2 * channels :]
    signal_all, filter_all = (
        lax.all_to_all(signal, ("row", "col"), split_axis=1, concat_axis=0, tiled=True),
        lax.all_to_all(long_filter, ("row", "col"), split_axis=1, concat_axis=0, tiled=True),
    )
    causal_all = local_causal(signal_all, filter_all)
    long_part = lax.all_to_all(causal_all, ("row", "col"), split_axis=0, concat_axis=1, tiled=True)
    mixed_out = gate_out * (long_part + skip_gain * signal)
    return mixed_out.astype(jnp.bfloat16)


def solution(mesh):
    in_specs = (
        P(("row", "col")),
        P(),
        P(),
        P(None, ("row", "col")),
        P(),
        P(("row", "col"), None),
        P(),
    )
    out_specs = P(("row", "col"), None)
    return jax.shard_map(local, mesh=mesh, in_specs=in_specs, out_specs=out_specs, check_vma=False)
```

profile of v0, /device:TPU:0, one launch (start us, length us, event | category | flops | bytes accessed | tf_op | source)
XLA Modules:
  0.0 561.6 jit_solution(3965734877258306150)
XLA Ops:
  6.5 5.3 fusion
  11.8 0.0 copy-done
  11.8 1.0 copy-done.6
  12.8 3.7 fusion.54
  16.5 0.0 all-gather.2.cloned.1.call-update
  16.5 0.0 copy-start.7
  16.5 3.0 copy.44
  19.5 11.7 %all-to-all-start.1 = ((f32[128,128,32]{0,2,1:T(8,128)}), f32[128,128,32]{0,2,1:T(8,128)}, u32[]{:S(2)}, u32[]{:S(2)}) async-start(f32[128,128,32]{0,2,1:T(8,128)} %bitcast.114), calls=%async_computation.1 | async-start | bytes 4194304 | tf_op jit(solution)/shard_map/all_to_all | solution.py:113
  31.2 0.0 copy-start.10
  31.2 0.5 fusion.101
  31.7 0.1 copy.49
  31.8 0.1 copy.47
  31.9 0.2 fusion.198
  32.2 30.5 %all-to-all-done.1 = f32[128,128,32]{0,2,1:T(8,128)} async-done(((f32[128,128,32]{0,2,1:T(8,128)}), f32[128,128,32]{0,2,1:T(8,128)}, u32[]{:S(2)}, u32[]{:S(2)}) %all-to-all-start.1) | async-done | bytes 2097184 | tf_op jit(solution)/shard_map/all_to_all | solution.py:113
  62.7 9.3 %fusion.38 = f32[256,128,32]{1,0,2:T(8,128)} fusion(f32[128,128,32]{0,2,1:T(8,128)} %all-to-all-done.1), kind=kOutput, calls=%fused_computation.58 | convolution fusion | flops 1611071488 | bytes 6291456 | tf_op jit(solution)/shard_map/sk,sjc->ckj/dot_general | solution.py:23
  71.9 281.6 %all-gather.2.cloned.1.call-done = bf16[512,12288]{0,1:T(8,128)(2,1)} async-done(((bf16[512,96]{0,1:T(8,128)(2,1)}), bf16[512,12288]{0,1:T(8,128)(2,1)}) %all-gather.2.cloned.1.call-update) | async-done | bytes 12582928 | tf_op jit(solution)/shard_map/all_gather | solution.py:31
  353.6 8.8 %convolution_convert_fusion = bf16[128,12288]{1,0:T(8,128)(2,1)S(1)} fusion(bf16[512,12288]{0,1:T(8,128)(2,1)} %all-gather.2.cloned.1.call-done, s32[128]{0:T(128)S(1)} %copy-done.10), kind=kOutput, calls=%fused_computation.5 | convolution fusion | flops 1612251136 | bytes 15729152 | tf_op jit(solution)/shard_map/dot_general | solution.py:104
  362.4 3.9 collective-permute-start
  366.3 9.3 %fusion.40 = f32[256,128,32]{1,0,2:T(8,128)} fusion(f32[128,128,32]{0,2,1:T(8,128)} %all-to-all-done.1), kind=kOutput, calls=%fused_computation.60 | convolution fusion | flops 1611071488 | bytes 6291456 | tf_op jit(solution)/shard_map/sk,sjc->ckj/dot_general | solution.py:23
  375.6 0.0 collective-permute-done
  375.6 0.9 maximum_convert_fusion
  376.5 5.2 fusion.7
  381.7 2.7 copy-done.4
  384.3 1.6 slice_multiply_fusion.7
  385.9 2.9 copy.40
  388.8 11.1 %all-to-all-start = ((f32[128,128,32]{0,2,1:T(8,128)}), f32[128,128,32]{0,2,1:T(8,128)}, u32[]{:S(2)}, u32[]{:S(2)}) async-start(f32[128,128,32]{0,2,1:T(8,128)} %bitcast.115), calls=%async_computation | async-start | bytes 4194304 | tf_op jit(solution)/shard_map/all_to_all | solution.py:112
  399.9 6.8 %fusion.13 = f32[32,256,128]{2,1,0:T(8,128)S(1)} fusion(f32[256,128,32]{1,0,2:T(8,128)} %fusion.40, f32[256,128,32]{1,0,2:T(8,128)} %fusion.38, f32[256,128]{1,0:T(8,128)S(1)} %copy.49, f32[256,128]{1,0:T(8,128)S(1)} %copy.47), kind=kOutput, calls=%fused_computation.22 | convolution fusion | flops 1615036416 | bytes 12845056 | tf_op jit(solution)/shard_map/jm,ckj->ckm/dot_general | solution.py:23
  406.7 4.2 fusion.15
  410.9 5.8 %fusion.34 = f32[32,256,128]{2,1,0:T(8,128)} fusion(f32[32,256,128]{2,1,0:T(8,128)S(1)} %fusion.13, f32[256,128,32]{1,0,2:T(8,128)S(1)} %copy-done.3, f32[256,128,32]{1,0,2:T(8,128)S(1)} %copy-done.2, f32[256,128]{1,0:T(8,128)S(1)} %copy.49, f32[256,128]{1,0:T(8,128)S(1)} %copy.47), kind=kOutput, calls=%fused_computation.50 | convolution fusion | flops 1616084992 | bytes 17039360 | tf_op jit(solution)/shard_map/jm,ckj->ckm/dot_general | solution.py:23
  416.7 5.8 %fusion.31 = f32[32,256,128]{2,1,0:T(8,128)} fusion(f32[32,256,128]{2,1,0:T(8,128)S(1)} %fusion.15, f32[256,128,32]{1,0,2:T(8,128)S(1)} %copy-done.3, f32[256,128,32]{1,0,2:T(8,128)S(1)} %copy-done.2, f32[256,128]{1,0:T(8,128)S(1)} %copy.49, f32[256,128]{1,0:T(8,128)S(1)} %copy.47), kind=kOutput, calls=%fused_computation.49 | convolution fusion | flops 1616084992 | bytes 17039360 | tf_op jit(solution)/shard_map/jm,ckj->ckm/dot_general | solution.py:23
  422.5 6.8 %all-to-all-done = f32[128,128,32]{0,2,1:T(8,128)} async-done(((f32[128,128,32]{0,2,1:T(8,128)}), f32[128,128,32]{0,2,1:T(8,128)}, u32[]{:S(2)}, u32[]{:S(2)}) %all-to-all-start) | async-done | bytes 2097184 | tf_op jit(solution)/shard_map/all_to_all | solution.py:112
  429.3 3.1 copy.41
  432.5 5.7 %fusion.42 = f32[128,32,256]{2,0,1:T(8,128)S(1)} fusion(f32[128,128,32]{1,0,2:T(8,128)} %copy.41), kind=kOutput, calls=%fused_computation.62 | convolution fusion | flops 1611071488 | bytes 6291456 | tf_op jit(solution)/shard_map/sk,sjc->ckj/dot_general | solution.py:23
  438.2 4.0 fusion.44
  442.2 9.4 %fusion.57 = f32[32,256,128]{2,1,0:T(8,128)} fusion(f32[128,32,256]{2,0,1:T(8,128)S(1)} %fusion.44, f32[128,32,256]{2,0,1:T(8,128)S(1)} %fusion.42, f32[256,128]{0,1:T(8,128)S(1)} %get-tuple-element.14, f32[256,128]{0,1:T(8,128)S(1)} %get-tuple-element.15), kind=kOutput, calls=%fused_computation.74 | convolution fusion | flops 1615036416 | bytes 12845056 | tf_op jit(solution)/shard_map/jm,ckj->ckm/dot_general | solution.py:23
  451.6 7.4 %fusion.61 = f32[32,256,128]{2,1,0:T(8,128)S(1)} fusion(f32[128,32,256]{2,0,1:T(8,128)S(1)} %fusion.44, f32[128,32,256]{2,0,1:T(8,128)S(1)} %fusion.42, f32[256,128]{0,1:T(8,128)S(1)} %get-tuple-element.14, f32[256,128]{0,1:T(8,128)S(1)} %get-tuple-element.15), kind=kOutput, calls=%fused_computation.75 | convolution fusion | flops 1615036416 | bytes 12845056 | tf_op jit(solution)/shard_map/jm,ckj->ckm/dot_general | solution.py:23
  459.0 9.1 %convolution_add_fusion.1 = f32[32,256,128]{2,1,0:T(8,128)} fusion(f32[32,256,128]{2,1,0:T(8,128)S(1)} %fusion.61, f32[128,32,256]{2,0,1:T(8,128)S(1)} %fusion.44, f32[128,32,256]{2,0,1:T(8,128)S(1)} %fusion.42, f32[256,128]{0,1:T(8,128)S(1)} %get-tuple-element.14, f32[256,128]{0,1:T(8,128)S(1)} %get-tuple-element.15), kind=kOutput, calls=%fused_computation.54 | convolution fusion | flops 1616084992 | bytes 17039360 | tf_op jit(solution)/shard_map/jm,ckj->ckm/dot_general | solution.py:23
  468.1 11.9 %multiply_add_fusion = (f32[32,256,128]{2,1,0:T(8,128)S(1)}, f32[32,256,128]{2,1,0:T(8,128)S(1)}) fusion(f32[32,256,128]{2,1,0:T(8,128)} %fusion.31, f32[32,256,128]{2,1,0:T(8,128)} %convolution_add_fusion.1, f32[32,256,128]{2,1,0:T(8,128)} %fusion.34, f32[32,256,128]{2,1,0:T(8,128)} %fusion.57, f32[128,32,256]{2,0,1:T(8,128)S(1)} %fusion.44, ...), kind=kOutput, calls=%fused_computation.44 | convolution fusion | flops 1622376448 | bytes 33816576 | tf_op jit(solution)/shard_map/jm,ckj->ckm/dot_general | solution.py:23
  480.1 4.2 fusion.91
  484.2 4.2 fusion.93
  488.4 4.9 convolution_add_fusion
  493.3 4.2 convolution_subtract_fusion
  497.6 4.2 fusion.23
  501.7 5.8 %multiply_bitcast_fusion = f32[128,128,32]{0,1,2:T(8,128)} fusion(f32[32,128,128]{2,1,0:T(8,128)S(1)} %fusion.23, f32[32,256,128]{1,2,0:T(8,128)S(1)} %convolution_add_fusion, f32[32,256,128]{1,2,0:T(8,128)S(1)} %convolution_subtract_fusion, f32[256,128]{0,1:T(8,128)S(1)} %get-tuple-element.14, f32[256,128]{0,1:T(8,128)S(1)} %get-tuple-element.15), kind=kOutput, calls=%fused_computation.66 | convolution fusion | flops 1615265792 | bytes 12845056 | tf_op jit(solution)/shard_map/sk,ckj->sjc/dot_general | solution.py:23
  507.5 3.1 copy.56
  510.7 35.6 %all_to_all.48 = f32[128,128,32]{1,2,0:T(8,128)} all-to-all(f32[128,128,32]{1,2,0:T(8,128)} %copy.56), channel_id=1, replica_groups=mesh['row'=16,'col'=8] {'row','col'}, dimensions={0} | all-to-all | bytes 4194304 | tf_op jit(solution)/shard_map/all_to_all | solution.py:116
  546.2 3.0 copy.57
  549.2 5.0 fusion.37
  (21 shorter events, 0.1 us)
Async XLA Ops:
  6.5 5.3 copy-start
  6.5 5.3 copy-start.9
  6.5 347.0 %all-gather.2.cloned.1.call-start = ((), (), s32[]{:S(2)}) async-start(), calls=%async_computation.3 | async-start | bytes 12681216 | tf_op jit(solution)/shard_map/all_gather | solution.py:31
  6.5 6.3 %copy-start.6 = (bf16[512,8192]{1,0:T(8,128)(2,1)S(1)}, bf16[512,8192]{1,0:T(8,128)(2,1)}, u32[]{:S(2)}) copy-start(bf16[512,8192]{1,0:T(8,128)(2,1)} %param.8) | copy-start | bytes 25165828
  16.5 15.4 %copy-start.7 = (f32[7,12288]{1,0:T(8,128)S(1)}, f32[7,12288]{1,0:T(8,128)}, u32[]{:S(2)}) copy-start(f32[7,12288]{1,0:T(8,128)} %param.11) | copy-start | bytes 1032196
  19.5 43.2 %all-to-all-start.1 = ((f32[128,128,32]{0,2,1:T(8,128)}), f32[128,128,32]{0,2,1:T(8,128)}, u32[]{:S(2)}, u32[]{:S(2)}) async-start(f32[128,128,32]{0,2,1:T(8,128)} %bitcast.114), calls=%async_computation.1 | async-start | bytes 4194304 | tf_op jit(solution)/shard_map/all_to_all | solution.py:113
  31.2 322.4 %copy-start.10 = (s32[128]{0:T(128)S(1)}, s32[128]{0:T(128)}, u32[]{:S(2)}) copy-start(s32[128]{0:T(128)} %param.7) | copy-start | bytes 1540
  362.4 13.2 %collective-permute-start = (bf16[6,12288]{1,0:T(8,128)(2,1)S(1)}, bf16[6,12288]{1,0:T(8,128)(2,1)S(1)}, u32[]{:S(2)}, u32[]{:S(2)}) collective-permute-start(bf16[6,12288]{1,0:T(8,128)(2,1)S(1)} %slice.72), channel_id=1, source_target_pairs={{0,1},{1,2},{2,3},{3,4},{4,5},{5,6},{6,7},{7,8},{8,9},{9,10},{10,1... | collective-permute-start | bytes 442376 | tf_op jit(solution)/shard_map/ppermute | solution.py:14
  381.7 2.7 copy-start.4
  388.8 40.5 %all-to-all-start = ((f32[128,128,32]{0,2,1:T(8,128)}), f32[128,128,32]{0,2,1:T(8,128)}, u32[]{:S(2)}, u32[]{:S(2)}) async-start(f32[128,128,32]{0,2,1:T(8,128)} %bitcast.115), calls=%async_computation | async-start | bytes 4194304 | tf_op jit(solution)/shard_map/all_to_all | solution.py:112
  399.9 6.8 %copy-start.2 = (f32[256,128,32]{1,0,2:T(8,128)S(1)}, f32[256,128,32]{1,0,2:T(8,128)}, u32[]{:S(2)}) copy-start(f32[256,128,32]{1,0,2:T(8,128)} %fusion.38) | copy-start | bytes 12582916
  399.9 6.8 %copy-start.3 = (f32[256,128,32]{1,0,2:T(8,128)S(1)}, f32[256,128,32]{1,0,2:T(8,128)}, u32[]{:S(2)}) copy-start(f32[256,128,32]{1,0,2:T(8,128)} %fusion.40) | copy-start | bytes 12582916
  432.4 5.7 %copy-start.5 = (f32[128,128,32]{1,0,2:T(8,128)S(1)}, f32[128,128,32]{1,0,2:T(8,128)}, u32[]{:S(2)}) copy-start(f32[128,128,32]{1,0,2:T(8,128)} %copy.41) | copy-start | bytes 6291460
  510.7 38.6 %copy-start.8 = (f32[4096]{0:T(1024)S(1)}, f32[4096]{0:T(1024)}, u32[]{:S(2)}) copy-start(f32[4096]{0:T(1024)} %param.13) | copy-start | bytes 49156
  546.2 8.1 %copy-start.1 = (bf16[8192,96]{0,1:T(8,128)(2,1)S(1)}, bf16[8192,96]{0,1:T(8,128)(2,1)}, u32[]{:S(2)}) copy-start(bf16[8192,96]{0,1:T(8,128)(2,1)} %param.10) | copy-start | bytes 4718596
Sparse Core Ops, SparseCore 0:
  16.6 336.8 all-gather.1
where the time goes:
time: 571 us; the launch traced here: 562 us
  waiting for transfers between devices  319 us (56%)
  matrix products  129 us (23%)
  blocking collectives  35.6 us (6%)
  starting transfers between devices  26.6 us (5%)
  local copies, waits for them, and re-layouts  19.3 us (3%)
  other arithmetic  18.4 us (3%)
  between operations  14.1 us (2%)
    all_gather x1, waiting for transfers between devices, project_table(): return lax.all_gather(own_columns, ('row', 'col'), axis=1, tiled=True)  282 us
    dot_general x18, matrix products, contract(): jnp.einsum(form, table_part, data_part, precision=lax.Precision.HIGHEST)  116 us
    all_to_all x1, blocking collectives, local(): lax.all_to_all(causal_all, ('row', 'col'), split_axis=0, concat_axis=1, t...  35.6 us
    all_to_all x1, waiting for transfers between devices, local(): lax.all_to_all(long_filter, ('row', 'col'), split_axis=1, concat_axis=0,...  30.5 us
    all_to_all x1, starting transfers between devices, local(): lax.all_to_all(long_filter, ('row', 'col'), split_axis=1, concat_axis=0,...  11.7 us
  transfers between devices with their start and end apart: 4, of which 3 were waited for; matrix products, arithmetic and copies ran while one was open for 8% of the time, Pallas kernels for 0%

commit v1 on v0

--- a/solution.py
+++ b/solution.py
@@ -6,6 +6,12 @@
 
 FFT_COLS = 128
 EPSILON = 1e-05
+
+
+def exchange_blocks(shard, axis, split, join):
+    pieces = jnp.split(shard, lax.axis_size(axis), axis=split)
+    incoming = lax.all_to_all(jnp.stack(pieces), axis, 0, 0)
+    return jnp.concatenate(incoming, axis=join)
 
 
 def passed_along(x, axis, by):
@@ -109,7 +115,7 @@
     gate_out = filtered[:, :channels]
     signal = filtered[:, channels : 2 * channels] * filtered[:, 2 * channels :]
     signal_all, filter_all = (
-        lax.all_to_all(signal, ("row", "col"), split_axis=1, concat_axis=0, tiled=True),
+        exchange_blocks(signal, ("row", "col"), 1, 0),
         lax.all_to_all(long_filter, ("row", "col"), split_axis=1, concat_axis=0, tiled=True),
     )
     causal_all = local_causal(signal_all, filter_all)

time: 571 us -> 815 us (1.43)
  local copies, waits for them, and re-layouts: 19.3 us -> 259 us
    another operation x0 -> x136, local copies, waits for them, and re-layouts: none -> 136 us  [exchange_blocks(): incoming = lax.all_to_all(jnp.stack(pieces), axis, 0, 0)]
    unnamed x23 -> x230, local copies, waits for them, and re-layouts: 6.64 us -> 114 us
  transfers between devices with their start and end apart: 4 -> 4, of which waited for: 3 -> 3; matrix products, arithmetic and copies ran while one was open for 8% -> 6% of each run, Pallas kernels for 0% -> 0%
where the time goes in v1:
time: 815 us; the launch traced here: 800 us
  waiting for transfers between devices  318 us (39%)
  local copies, waits for them, and re-layouts  259 us (32%)
  matrix products  129 us (16%)
  blocking collectives  35.4 us (4%)
  starting transfers between devices  27.1 us (3%)
  other arithmetic  17.2 us (2%)
  between operations  14.4 us (2%)
    all_gather x1, waiting for transfers between devices, project_table(): return lax.all_gather(own_columns, ('row', 'col'), axis=1, tiled=True)  281 us
    another operation x136, local copies, waits for them, and re-layouts, exchange_blocks(): incoming = lax.all_to_all(jnp.stack(pieces), axis, 0, 0)  136 us
    dot_general x18, matrix products, contract(): jnp.einsum(form, table_part, data_part, precision=lax.Precision.HIGHEST)  116 us
    unnamed x230, local copies, waits for them, and re-layouts  114 us
    all_to_all x1, blocking collectives, local(): lax.all_to_all(causal_all, ('row', 'col'), split_axis=0, concat_axis=1, t...  35.4 us
    all_to_all x1, waiting for transfers between devices, local(): lax.all_to_all(long_filter, ('row', 'col'), split_axis=1, concat_axis=0,...  30.5 us
  transfers between devices with their start and end apart: 4, of which 3 were waited for; matrix products, arithmetic and copies ran while one was open for 6% of the time, Pallas kernels for 0%

profile of v1, /device:TPU:0, one launch (start us, length us, event | category | flops | bytes accessed | tf_op | source)
XLA Modules:
  0.0 800.4 jit_solution(3122146740892923633)
XLA Ops:
  6.5 5.3 fusion
  12.8 3.7 fusion.50
  16.5 2.9 copy.173
  19.4 11.7 %all-to-all-start.1 = ((f32[128,128,32]{0,2,1:T(8,128)}), f32[128,128,32]{0,2,1:T(8,128)}, u32[]{:S(2)}, u32[]{:S(2)}) async-start(f32[128,128,32]{0,2,1:T(8,128)} %bitcast.366), calls=%async_computation.1 | async-start | bytes 4194304 | tf_op jit(solution)/shard_map/all_to_all | solution.py:119
  32.1 30.5 %all-to-all-done.1 = f32[128,128,32]{0,2,1:T(8,128)} async-done(((f32[128,128,32]{0,2,1:T(8,128)}), f32[128,128,32]{0,2,1:T(8,128)}, u32[]{:S(2)}, u32[]{:S(2)}) %all-to-all-start.1) | async-done | bytes 2097184 | tf_op jit(solution)/shard_map/all_to_all | solution.py:119
  62.6 9.3 %fusion.38 = f32[256,128,32]{1,0,2:T(8,128)} fusion(f32[128,128,32]{0,2,1:T(8,128)} %all-to-all-done.1), kind=kOutput, calls=%fused_computation.58 | convolution fusion | flops 1611071488 | bytes 6291456 | tf_op jit(solution)/shard_map/sk,sjc->ckj/dot_general | solution.py:29
  71.9 281.2 %all-gather.2.cloned.1.call-done = bf16[512,12288]{0,1:T(8,128)(2,1)} async-done(((bf16[512,96]{0,1:T(8,128)(2,1)}), bf16[512,12288]{0,1:T(8,128)(2,1)}) %all-gather.2.cloned.1.call-update) | async-done | bytes 12582928 | tf_op jit(solution)/shard_map/all_gather | solution.py:37
  353.1 8.8 %convolution_convert_fusion = bf16[128,12288]{1,0:T(8,128)(2,1)S(1)} fusion(bf16[512,12288]{0,1:T(8,128)(2,1)} %all-gather.2.cloned.1.call-done, s32[128]{0:T(128)S(1)} %copy-done.50), kind=kOutput, calls=%fused_computation.5 | convolution fusion | flops 1612251136 | bytes 15729152 | tf_op jit(solution)/shard_map/dot_general | solution.py:110
  361.9 4.0 collective-permute-start
  365.9 9.4 %fusion.40 = f32[256,128,32]{1,0,2:T(8,128)} fusion(f32[128,128,32]{0,2,1:T(8,128)} %all-to-all-done.1), kind=kOutput, calls=%fused_computation.60 | convolution fusion | flops 1611071488 | bytes 6291456 | tf_op jit(solution)/shard_map/sk,sjc->ckj/dot_general | solution.py:29
  376.2 5.2 fusion.7
  381.6 2.4 copy-done.4
  392.8 1.5 copy.53
  407.9 1.5 copy.43
  411.0 1.5 copy.41
  432.1 1.5 copy.117
  442.1 1.5 copy.148
  443.6 1.5 copy.147
  445.1 1.5 copy.146
  455.7 1.5 copy.139
  457.2 1.5 copy.138
  466.3 1.5 copy.132
  467.8 1.5 copy.131
  476.9 1.5 copy.87
  484.5 1.5 copy.82
  627.3 11.5 %all-to-all-start = ((f32[128,128,32]{1,2,0:T(8,128)}), f32[128,128,32]{1,2,0:T(8,128)}, u32[]{:S(2)}, u32[]{:S(2)}) async-start(f32[128,128,32]{1,2,0:T(8,128)} %constant_dynamic-update-slice_fusion), calls=%async_computation | async-start | bytes 4194304 | tf_op jit(solution)/shard_map/all_to_all | solution.py:13
  638.7 6.8 fusion.13
  645.5 4.2 fusion.15
  649.8 5.8 fusion.34
  655.6 5.8 fusion.31
  661.4 6.7 all-to-all-done
  668.1 3.1 copy.169
  671.3 5.7 fusion.67
  677.0 4.0 fusion.71
  681.0 9.4 %fusion.53 = f32[32,256,128]{2,1,0:T(8,128)} fusion(f32[128,32,256]{2,0,1:T(8,128)S(1)} %fusion.71, f32[128,32,256]{2,0,1:T(8,128)S(1)} %fusion.67, f32[256,128]{0,1:T(8,128)S(1)} %get-tuple-element.142, f32[256,128]{0,1:T(8,128)S(1)} %get-tuple-element.143), kind=kOutput, calls=%fused_computation.70 | convolution fusion | flops 1615036416 | bytes 12845056 | tf_op jit(solution)/shard_map/jm,ckj->ckm/dot_general | solution.py:29
  690.4 7.4 fusion.57
  697.8 9.2 %convolution_add_fusion.1 = f32[32,256,128]{2,1,0:T(8,128)} fusion(f32[32,256,128]{2,1,0:T(8,128)S(1)} %fusion.57, f32[128,32,256]{2,0,1:T(8,128)S(1)} %fusion.71, f32[128,32,256]{2,0,1:T(8,128)S(1)} %fusion.67, f32[256,128]{0,1:T(8,128)S(1)} %get-tuple-element.142, f32[256,128]{0,1:T(8,128)S(1)} %get-tuple-element.143), kind=kOutput, calls=%fused_computation.54 | convolution fusion | flops 1616084992 | bytes 17039360 | tf_op jit(solution)/shard_map/jm,ckj->ckm/dot_general | solution.py:29
  707.0 11.9 %multiply_add_fusion = (f32[32,256,128]{2,1,0:T(8,128)S(1)}, f32[32,256,128]{2,1,0:T(8,128)S(1)}) fusion(f32[32,256,128]{2,1,0:T(8,128)} %fusion.31, f32[32,256,128]{2,1,0:T(8,128)} %convolution_add_fusion.1, f32[32,256,128]{2,1,0:T(8,128)} %fusion.34, f32[32,256,128]{2,1,0:T(8,128)} %fusion.53, f32[128,32,256]{2,0,1:T(8,128)S(1)} %fusion.71, ...), kind=kOutput, calls=%fused_computation.44 | convolution fusion | flops 1622376448 | bytes 33816576 | tf_op jit(solution)/shard_map/jm,ckj->ckm/dot_general | solution.py:29
  719.0 4.2 fusion.89
  723.2 4.2 fusion.91
  727.4 4.9 convolution_add_fusion
  732.3 4.2 convolution_subtract_fusion
  736.5 4.2 fusion.23
  740.7 5.7 multiply_bitcast_fusion
  746.4 3.1 copy.185
  749.5 35.4 %all_to_all.37 = f32[128,128,32]{1,2,0:T(8,128)} all-to-all(f32[128,128,32]{1,2,0:T(8,128)} %copy.185), channel_id=1, replica_groups=mesh['row'=16,'col'=8] {'row','col'}, dimensions={0} | all-to-all | bytes 4194304 | tf_op jit(solution)/shard_map/all_to_all | solution.py:122
  785.0 3.0 copy.186
  788.0 5.1 fusion.37
  (363 shorter events, 226.4 us)
Async XLA Ops:
  6.5 346.6 %all-gather.2.cloned.1.call-start = ((), (), s32[]{:S(2)}) async-start(), calls=%async_computation.3 | async-start | bytes 12681216 | tf_op jit(solution)/shard_map/all_gather | solution.py:37
  19.4 12.4 %copy-start.7 = (f32[7,12288]{1,0:T(8,128)S(1)}, f32[7,12288]{1,0:T(8,128)}, u32[]{:S(2)}) copy-start(f32[7,12288]{1,0:T(8,128)} %param.11) | copy-start | bytes 1032196
  19.4 43.2 %all-to-all-start.1 = ((f32[128,128,32]{0,2,1:T(8,128)}), f32[128,128,32]{0,2,1:T(8,128)}, u32[]{:S(2)}, u32[]{:S(2)}) async-start(f32[128,128,32]{0,2,1:T(8,128)} %bitcast.366), calls=%async_computation.1 | async-start | bytes 4194304 | tf_op jit(solution)/shard_map/all_to_all | solution.py:119
  32.1 321.0 %copy-start.50 = (s32[128]{0:T(128)S(1)}, s32[128]{0:T(128)}, u32[]{:S(2)}) copy-start(s32[128]{0:T(128)} %param.7) | copy-start | bytes 1540
  361.9 13.4 %collective-permute-start = (bf16[6,12288]{1,0:T(8,128)(2,1)S(1)}, bf16[6,12288]{1,0:T(8,128)(2,1)S(1)}, u32[]{:S(2)}, u32[]{:S(2)}) collective-permute-start(bf16[6,12288]{1,0:T(8,128)(2,1)S(1)} %slice.72), channel_id=1, source_target_pairs={{0,1},{1,2},{2,3},{3,4},{4,5},{5,6},{6,7},{7,8},{8,9},{9,10},{10,1... | collective-permute-start | bytes 442376 | tf_op jit(solution)/shard_map/ppermute | solution.py:20
  514.5 22.1 %copy-start.47 = (f32[1,128,32]{1,2,0:T(8,128)S(1)}, f32[1,128,32]{1,2,0:T(8,128)}, u32[]{:S(2)}) copy-start(f32[1,128,32]{1,2,0:T(8,128)} %copy.54) | copy-start | bytes 49156
  517.1 63.2 %copy-start.46 = (f32[1,128,32]{1,2,0:T(8,128)S(1)}, f32[1,128,32]{1,2,0:T(8,128)}, u32[]{:S(2)}) copy-start(f32[1,128,32]{1,2,0:T(8,128)} %copy.91) | copy-start | bytes 49156
  517.1 63.8 %copy-start.45 = (f32[1,128,32]{1,2,0:T(8,128)S(1)}, f32[1,128,32]{1,2,0:T(8,128)}, u32[]{:S(2)}) copy-start(f32[1,128,32]{1,2,0:T(8,128)} %copy.92) | copy-start | bytes 49156
  517.7 75.2 %copy-start.44 = (f32[1,128,32]{1,2,0:T(8,128)S(1)}, f32[1,128,32]{1,2,0:T(8,128)}, u32[]{:S(2)}) copy-start(f32[1,128,32]{1,2,0:T(8,128)} %copy.112) | copy-start | bytes 49156
  517.7 75.8 %copy-start.43 = (f32[1,128,32]{1,2,0:T(8,128)S(1)}, f32[1,128,32]{1,2,0:T(8,128)}, u32[]{:S(2)}) copy-start(f32[1,128,32]{1,2,0:T(8,128)} %copy.113) | copy-start | bytes 49156
  517.8 76.4 %copy-start.42 = (f32[1,128,32]{1,2,0:T(8,128)S(1)}, f32[1,128,32]{1,2,0:T(8,128)}, u32[]{:S(2)}) copy-start(f32[1,128,32]{1,2,0:T(8,128)} %copy.114) | copy-start | bytes 49156
  517.8 77.0 %copy-start.41 = (f32[1,128,32]{1,2,0:T(8,128)S(1)}, f32[1,128,32]{1,2,0:T(8,128)}, u32[]{:S(2)}) copy-start(f32[1,128,32]{1,2,0:T(8,128)} %copy.115) | copy-start | bytes 49156
  517.8 77.6 %copy-start.39 = (f32[1,128,32]{1,2,0:T(8,128)S(1)}, f32[1,128,32]{1,2,0:T(8,128)}, u32[]{:S(2)}) copy-start(f32[1,128,32]{1,2,0:T(8,128)} %copy.116) | copy-start | bytes 49156
  517.8 78.1 %copy-start.37 = (f32[1,128,32]{1,2,0:T(8,128)S(1)}, f32[1,128,32]{1,2,0:T(8,128)}, u32[]{:S(2)}) copy-start(f32[1,128,32]{1,2,0:T(8,128)} %copy.117) | copy-start | bytes 49156
  517.8 78.7 %copy-start.35 = (f32[1,128,32]{1,2,0:T(8,128)S(1)}, f32[1,128,32]{1,2,0:T(8,128)}, u32[]{:S(2)}) copy-start(f32[1,128,32]{1,2,0:T(8,128)} %copy.118) | copy-start | bytes 49156
  517.8 79.3 %copy-start.33 = (f32[1,128,32]{1,2,0:T(8,128)S(1)}, f32[1,128,32]{1,2,0:T(8,128)}, u32[]{:S(2)}) copy-start(f32[1,128,32]{1,2,0:T(8,128)} %copy.119) | copy-start | bytes 49156
  517.9 79.8 %copy-start.31 = (f32[1,128,32]{1,2,0:T(8,128)S(1)}, f32[1,128,32]{1,2,0:T(8,128)}, u32[]{:S(2)}) copy-start(f32[1,128,32]{1,2,0:T(8,128)} %copy.120) | copy-start | bytes 49156
  517.9 80.4 %copy-start.29 = (f32[1,128,32]{1,2,0:T(8,128)S(1)}, f32[1,128,32]{1,2,0:T(8,128)}, u32[]{:S(2)}) copy-start(f32[1,128,32]{1,2,0:T(8,128)} %copy.121) | copy-start | bytes 49156
  518.0 80.9 %copy-start.27 = (f32[1,128,32]{1,2,0:T(8,128)S(1)}, f32[1,128,32]{1,2,0:T(8,128)}, u32[]{:S(2)}) copy-start(f32[1,128,32]{1,2,0:T(8,128)} %copy.122) | copy-start | bytes 49156
  518.0 81.5 %copy-start.25 = (f32[1,128,32]{1,2,0:T(8,128)S(1)}, f32[1,128,32]{1,2,0:T(8,128)}, u32[]{:S(2)}) copy-start(f32[1,128,32]{1,2,0:T(8,128)} %copy.123) | copy-start | bytes 49156
  518.0 82.1 %copy-start.23 = (f32[1,128,32]{1,2,0:T(8,128)S(1)}, f32[1,128,32]{1,2,0:T(8,128)}, u32[]{:S(2)}) copy-start(f32[1,128,32]{1,2,0:T(8,128)} %copy.124) | copy-start | bytes 49156
  518.1 82.7 %copy-start.21 = (f32[1,128,32]{1,2,0:T(8,128)S(1)}, f32[1,128,32]{1,2,0:T(8,128)}, u32[]{:S(2)}) copy-start(f32[1,128,32]{1,2,0:T(8,128)} %copy.125) | copy-start | bytes 49156
  518.1 83.3 %copy-start.19 = (f32[1,128,32]{1,2,0:T(8,128)S(1)}, f32[1,128,32]{1,2,0:T(8,128)}, u32[]{:S(2)}) copy-start(f32[1,128,32]{1,2,0:T(8,128)} %copy.126) | copy-start | bytes 49156
  518.2 83.8 %copy-start.17 = (f32[1,128,32]{1,2,0:T(8,128)S(1)}, f32[1,128,32]{1,2,0:T(8,128)}, u32[]{:S(2)}) copy-start(f32[1,128,32]{1,2,0:T(8,128)} %copy.127) | copy-start | bytes 49156
  518.2 84.4 %copy-start.15 = (f32[1,128,32]{1,2,0:T(8,128)S(1)}, f32[1,128,32]{1,2,0:T(8,128)}, u32[]{:S(2)}) copy-start(f32[1,128,32]{1,2,0:T(8,128)} %copy.128) | copy-start | bytes 49156
  518.2 85.0 %copy-start.13 = (f32[1,128,32]{1,2,0:T(8,128)S(1)}, f32[1,128,32]{1,2,0:T(8,128)}, u32[]{:S(2)}) copy-start(f32[1,128,32]{1,2,0:T(8,128)} %copy.129) | copy-start | bytes 49156
  518.3 85.5 %copy-start.11 = (f32[1,128,32]{1,2,0:T(8,128)S(1)}, f32[1,128,32]{1,2,0:T(8,128)}, u32[]{:S(2)}) copy-start(f32[1,128,32]{1,2,0:T(8,128)} %copy.130) | copy-start | bytes 49156
  518.3 86.1 %copy-start.40 = (f32[1,128,32]{1,2,0:T(8,128)S(1)}, f32[1,128,32]{1,2,0:T(8,128)}, u32[]{:S(2)}) copy-start(f32[1,128,32]{1,2,0:T(8,128)} %copy.131) | copy-start | bytes 49156
  518.3 86.6 %copy-start.38 = (f32[1,128,32]{1,2,0:T(8,128)S(1)}, f32[1,128,32]{1,2,0:T(8,128)}, u32[]{:S(2)}) copy-start(f32[1,128,32]{1,2,0:T(8,128)} %copy.132) | copy-start | bytes 49156
  518.3 87.3 %copy-start.36 = (f32[1,128,32]{1,2,0:T(8,128)S(1)}, f32[1,128,32]{1,2,0:T(8,128)}, u32[]{:S(2)}) copy-start(f32[1,128,32]{1,2,0:T(8,128)} %copy.133) | copy-start | bytes 49156
  518.3 87.9 %copy-start.34 = (f32[1,128,32]{1,2,0:T(8,128)S(1)}, f32[1,128,32]{1,2,0:T(8,128)}, u32[]{:S(2)}) copy-start(f32[1,128,32]{1,2,0:T(8,128)} %copy.134) | copy-start | bytes 49156
  518.4 88.4 %copy-start.32 = (f32[1,128,32]{1,2,0:T(8,128)S(1)}, f32[1,128,32]{1,2,0:T(8,128)}, u32[]{:S(2)}) copy-start(f32[1,128,32]{1,2,0:T(8,128)} %copy.135) | copy-start | bytes 49156
  518.4 89.0 %copy-start.30 = (f32[1,128,32]{1,2,0:T(8,128)S(1)}, f32[1,128,32]{1,2,0:T(8,128)}, u32[]{:S(2)}) copy-start(f32[1,128,32]{1,2,0:T(8,128)} %copy.136) | copy-start | bytes 49156
  518.4 89.6 %copy-start.28 = (f32[1,128,32]{1,2,0:T(8,128)S(1)}, f32[1,128,32]{1,2,0:T(8,128)}, u32[]{:S(2)}) copy-start(f32[1,128,32]{1,2,0:T(8,128)} %copy.137) | copy-start | bytes 49156
  518.5 90.1 %copy-start.26 = (f32[1,128,32]{1,2,0:T(8,128)S(1)}, f32[1,128,32]{1,2,0:T(8,128)}, u32[]{:S(2)}) copy-start(f32[1,128,32]{1,2,0:T(8,128)} %copy.138) | copy-start | bytes 49156
  518.5 90.7 %copy-start.24 = (f32[1,128,32]{1,2,0:T(8,128)S(1)}, f32[1,128,32]{1,2,0:T(8,128)}, u32[]{:S(2)}) copy-start(f32[1,128,32]{1,2,0:T(8,128)} %copy.139) | copy-start | bytes 49156
  518.6 91.2 %copy-start.22 = (f32[1,128,32]{1,2,0:T(8,128)S(1)}, f32[1,128,32]{1,2,0:T(8,128)}, u32[]{:S(2)}) copy-start(f32[1,128,32]{1,2,0:T(8,128)} %copy.140) | copy-start | bytes 49156
  518.6 91.8 %copy-start.20 = (f32[1,128,32]{1,2,0:T(8,128)S(1)}, f32[1,128,32]{1,2,0:T(8,128)}, u32[]{:S(2)}) copy-start(f32[1,128,32]{1,2,0:T(8,128)} %copy.141) | copy-start | bytes 49156
  518.6 92.4 %copy-start.18 = (f32[1,128,32]{1,2,0:T(8,128)S(1)}, f32[1,128,32]{1,2,0:T(8,128)}, u32[]{:S(2)}) copy-start(f32[1,128,32]{1,2,0:T(8,128)} %copy.142) | copy-start | bytes 49156
  518.7 93.0 %copy-start.16 = (f32[1,128,32]{1,2,0:T(8,128)S(1)}, f32[1,128,32]{1,2,0:T(8,128)}, u32[]{:S(2)}) copy-start(f32[1,128,32]{1,2,0:T(8,128)} %copy.143) | copy-start | bytes 49156
  518.7 93.6 %copy-start.14 = (f32[1,128,32]{1,2,0:T(8,128)S(1)}, f32[1,128,32]{1,2,0:T(8,128)}, u32[]{:S(2)}) copy-start(f32[1,128,32]{1,2,0:T(8,128)} %copy.144) | copy-start | bytes 49156
  518.7 94.1 %copy-start.12 = (f32[1,128,32]{1,2,0:T(8,128)S(1)}, f32[1,128,32]{1,2,0:T(8,128)}, u32[]{:S(2)}) copy-start(f32[1,128,32]{1,2,0:T(8,128)} %copy.145) | copy-start | bytes 49156
  518.7 94.7 %copy-start.10 = (f32[1,128,32]{1,2,0:T(8,128)S(1)}, f32[1,128,32]{1,2,0:T(8,128)}, u32[]{:S(2)}) copy-start(f32[1,128,32]{1,2,0:T(8,128)} %copy.146) | copy-start | bytes 49156
  518.7 95.3 %copy-start.9 = (f32[1,128,32]{1,2,0:T(8,128)S(1)}, f32[1,128,32]{1,2,0:T(8,128)}, u32[]{:S(2)}) copy-start(f32[1,128,32]{1,2,0:T(8,128)} %copy.147) | copy-start | bytes 49156
  518.8 95.8 %copy-start.8 = (f32[1,128,32]{1,2,0:T(8,128)S(1)}, f32[1,128,32]{1,2,0:T(8,128)}, u32[]{:S(2)}) copy-start(f32[1,128,32]{1,2,0:T(8,128)} %copy.148) | copy-start | bytes 49156
  627.3 40.9 %all-to-all-start = ((f32[128,128,32]{1,2,0:T(8,128)}), f32[128,128,32]{1,2,0:T(8,128)}, u32[]{:S(2)}, u32[]{:S(2)}) async-start(f32[128,128,32]{1,2,0:T(8,128)} %constant_dynamic-update-slice_fusion), calls=%async_computation | async-start | bytes 4194304 | tf_op jit(solution)/shard_map/all_to_all | solution.py:13
  638.7 6.8 copy-start.2
  638.7 6.8 copy-start.3
  (7 other events, 33.4 us)
Sparse Core Ops, SparseCore 0:
  16.6 336.4 all-gather.1
